TPU v7x, 32 devices: a whole 2x2x4 slice. The times are simulated.
32 devices in a mesh: dp: 4 (over y, core), fsdp: 8 (over z, x).
Axes of the slice: x: 2, y: 2, z: 4, core: 2. Of those that a mesh axis runs over, the one named last changes fastest.
Arguments:
- frames: bfloat16 [16384, 768], P(('dp', 'fsdp')), may hold values from -6 to 6
- lengths: int32 [32, 2], P(('dp', 'fsdp')), may hold values from 0 to 512, as said below
- query_weight: bfloat16 [768, 768], P(('dp', 'fsdp')), may hold values from -0.21875 to 0.21875
- query_bias: bfloat16 [768], P(('dp', 'fsdp')), may hold values from -3 to 3
- key_weight: bfloat16 [768, 768], P(('dp', 'fsdp')), may hold values from -0.21875 to 0.21875
- value_weight: bfloat16 [768, 768], P(('dp', 'fsdp')), may hold values from -0.21875 to 0.21875
- value_bias: bfloat16 [768], P(('dp', 'fsdp')), may hold values from -3 to 3
- output_weight: bfloat16 [768, 768], P(('dp', 'fsdp')), may hold values from -2.5 to 2.5
- output_bias: bfloat16 [768], P(('dp', 'fsdp')), may hold values from -3 to 3
- first_gain: bfloat16 [768], P(('dp', 'fsdp')), may hold values from 0.5 to 1.5
- first_shift: bfloat16 [768], P(('dp', 'fsdp')), may hold values from -3 to 3
- inner_weight: bfloat16 [768, 3072], P(('dp', 'fsdp')), may hold values from -0.21875 to 0.21875
- inner_bias: bfloat16 [3072], P(('dp', 'fsdp')), may hold values from -3 to 3
- outer_weight: bfloat16 [3072, 768], P(('dp', 'fsdp')), may hold values from -0.109375 to 0.109375
- outer_bias: bfloat16 [768], P(('dp', 'fsdp')), may hold values from -3 to 3
- second_gain: bfloat16 [768], P(('dp', 'fsdp')), may hold values from 0.5 to 1.5
- second_shift: bfloat16 [768], P(('dp', 'fsdp')), may hold values from -3 to 3
- grad_out: bfloat16 [16384, 768], P(('dp', 'fsdp')), may hold values from -6 to 6
Outputs:
- layer_out: bfloat16 [16384, 768], P(('dp', 'fsdp'))
- frames_grad: bfloat16 [16384, 768], P(('dp', 'fsdp'))
- query_weight_grad: float32 [768, 768], P(('dp', 'fsdp'))
- query_bias_grad: float32 [768], P(('dp', 'fsdp'))
- key_weight_grad: float32 [768, 768], P(('dp', 'fsdp'))
- value_weight_grad: float32 [768, 768], P(('dp', 'fsdp'))
- value_bias_grad: float32 [768], P(('dp', 'fsdp'))
- output_weight_grad: float32 [768, 768], P(('dp', 'fsdp'))
- output_bias_grad: float32 [768], P(('dp', 'fsdp'))
- first_gain_grad: float32 [768], P(('dp', 'fsdp'))
- first_shift_grad: float32 [768], P(('dp', 'fsdp'))
- inner_weight_grad: float32 [768, 3072], P(('dp', 'fsdp'))
- inner_bias_grad: float32 [3072], P(('dp', 'fsdp'))
- outer_weight_grad: float32 [3072, 768], P(('dp', 'fsdp'))
- outer_bias_grad: float32 [768], P(('dp', 'fsdp'))
- second_gain_grad: float32 [768], P(('dp', 'fsdp'))
- second_shift_grad: float32 [768], P(('dp', 'fsdp'))
Inputs may be any that keep to these rules, and one draw needn't show every extreme that they name: `lengths`: row b holds block b's two utterances: slot 0 has 100 to 512 frames, slot 1 has 0 (empty) up to 512 minus slot 0; the block's remaining slots are padding. In one block, drawn from the seed, slot 0 fills all 512 slots.
All inputs are finite; a program needn't handle non-finite values.
Results may differ from a plain program's by a relative error of at most 0.015.
Values may be sent and summed in bfloat16 or wider, within the bound.
A program may use at most 192 MiB of HBM per device.

v0:
```python
import jax
import jax.numpy as jnp
from jax import lax
from jax.sharding import PartitionSpec as P

HEADS = 12


def layer_norm(values, gain_vec, shift_vec):
    center = values - jnp.mean(values, axis=-1, keepdims=True)
    spread = jnp.mean(center * center, axis=-1, keepdims=True)
    return center * lax.rsqrt(spread + 1e-05) * gain_vec + shift_vec


def exact_gelu(values):
    return jax.nn.gelu(values, approximate=False)


def matmul(left_side, right_side):
    return jnp.dot(left_side, right_side, preferred_element_type=jnp.float32)


def matmul_tn(left_side, right_side):
    return lax.dot_general(
        left_side, right_side, (((0,), (0,)), ((), ())), preferred_element_type=jnp.float32
    )


def matmul_nt(left_side, right_side):
    return lax.dot_general(
        left_side, right_side, (((1,), (1,)), ((), ())), preferred_element_type=jnp.float32
    )


def column_sums(values):
    return jnp.sum(values.astype(jnp.float32), axis=0)


def block_scores(query_block, key_heads, group_block, groups, score_scale):
    raw_scores = (
        jnp.einsum("qhd,khd->hqk", query_block, key_heads, preferred_element_type=jnp.float32)
        * score_scale
    )
    allowed = group_block[:, None] == groups[None, :]
    return jnp.where(allowed[None], raw_scores, -1e30)


def per_device(
    frames,
    lengths,
    query_weight,
    query_bias,
    key_weight,
    value_weight,
    value_bias,
    output_weight,
    output_bias,
    first_gain,
    first_shift,
    inner_weight,
    inner_bias,
    outer_weight,
    outer_bias,
    second_gain,
    second_shift,
    grad_out,
):
    frame_count = frames.shape[0]
    model_width = frames.shape[1]
    head_size = model_width // HEADS
    score_scale = head_size ** (-0.5)
    places = jnp.arange(frame_count, dtype=jnp.int32)
    bounds = jnp.cumsum(lengths[0])
    groups = jnp.sum((places[:, None] >= bounds[None, :]).astype(jnp.int32), axis=1)
    live_mask = (places < bounds[-1]).astype(jnp.float32)
    gathered = (
        lax.all_gather(query_weight, ("dp", "fsdp"), axis=0, tiled=True),
        lax.all_gather(query_bias, ("dp", "fsdp"), axis=0, tiled=True),
        lax.all_gather(key_weight, ("dp", "fsdp"), axis=0, tiled=True),
        lax.all_gather(value_weight, ("dp", "fsdp"), axis=0, tiled=True),
        lax.all_gather(value_bias, ("dp", "fsdp"), axis=0, tiled=True),
        lax.all_gather(output_weight, ("dp", "fsdp"), axis=0, tiled=True),
        lax.all_gather(output_bias, ("dp", "fsdp"), axis=0, tiled=True),
        lax.all_gather(first_gain, ("dp", "fsdp"), axis=0, tiled=True),
        lax.all_gather(first_shift, ("dp", "fsdp"), axis=0, tiled=True),
        lax.all_gather(inner_weight, ("dp", "fsdp"), axis=0, tiled=True),
        lax.all_gather(inner_bias, ("dp", "fsdp"), axis=0, tiled=True),
        lax.all_gather(outer_weight, ("dp", "fsdp"), axis=0, tiled=True),
        lax.all_gather(outer_bias, ("dp", "fsdp"), axis=0, tiled=True),
        lax.all_gather(second_gain, ("dp", "fsdp"), axis=0, tiled=True),
        lax.all_gather(second_shift, ("dp", "fsdp"), axis=0, tiled=True),
    )
    (
        query_mat,
        query_vec,
        key_mat,
        value_mat,
        value_vec,
        output_mat,
        output_vec,
        first_scale,
        first_offset,
        inner_mat,
        inner_vec,
        outer_mat,
        outer_vec,
        second_scale,
        second_offset,
    ) = gathered
    query_rows = (matmul(frames, query_mat) + query_vec.astype(jnp.float32)).astype(jnp.bfloat16)
    key_rows = matmul(frames, key_mat).astype(jnp.bfloat16)
    value_rows = (matmul(frames, value_mat) + value_vec.astype(jnp.float32)).astype(jnp.bfloat16)
    query_heads = query_rows.reshape(frame_count, HEADS, head_size)
    key_heads = key_rows.reshape(frame_count, HEADS, head_size)
    value_heads = value_rows.reshape(frame_count, HEADS, head_size)
    scores = block_scores(query_heads, key_heads, groups, groups, score_scale)
    row_max = jnp.max(scores, axis=-1, keepdims=True)
    raw_weights = jnp.exp(scores - row_max)
    row_total = jnp.sum(raw_weights, axis=-1, keepdims=True)
    attn_prob = raw_weights / row_total
    log_totals = row_max + jnp.log(row_total)
    context_parts = jnp.einsum(
        "hqk,khd->qhd",
        attn_prob.astype(jnp.bfloat16),
        value_heads,
        preferred_element_type=jnp.float32,
    )
    context_rows = context_parts.reshape(frame_count, model_width).astype(jnp.bfloat16)
    frames_float = frames.astype(jnp.float32)
    resid_one = frames_float + matmul(context_rows, output_mat) + output_vec.astype(jnp.float32)
    hidden, first_pull = jax.vjp(
        layer_norm, resid_one, first_scale.astype(jnp.float32), first_offset.astype(jnp.float32)
    )
    hidden_low = hidden.astype(jnp.bfloat16)
    inner_pre = matmul(hidden_low, inner_mat) + inner_vec.astype(jnp.float32)
    active, gelu_pull = jax.vjp(exact_gelu, inner_pre)
    active_low = active.astype(jnp.bfloat16)
    outer_out = matmul(active_low, outer_mat) + outer_vec.astype(jnp.float32)
    normed_out, second_pull = jax.vjp(
        layer_norm,
        hidden + outer_out,
        second_scale.astype(jnp.float32),
        second_offset.astype(jnp.float32),
    )
    layer_out = (normed_out * live_mask[:, None]).astype(jnp.bfloat16)
    regathered = (
        lax.all_gather(query_weight, ("dp", "fsdp"), axis=0, tiled=True),
        lax.all_gather(key_weight, ("dp", "fsdp"), axis=0, tiled=True),
        lax.all_gather(value_weight, ("dp", "fsdp"), axis=0, tiled=True),
        lax.all_gather(output_weight, ("dp", "fsdp"), axis=0, tiled=True),
        lax.all_gather(inner_weight, ("dp", "fsdp"), axis=0, tiled=True),
        lax.all_gather(outer_weight, ("dp", "fsdp"), axis=0, tiled=True),
    )
    query_mat, key_mat, value_mat, output_mat, inner_mat, outer_mat = regathered
    grad_top = grad_out.astype(jnp.float32) * live_mask[:, None]
    grad_two, second_gain_grad, second_shift_grad = second_pull(grad_top)
    grad_outer = grad_two.astype(jnp.bfloat16)
    outer_mat_grad = matmul_tn(active_low, grad_outer)
    outer_vec_grad = column_sums(grad_outer)
    (grad_inner,) = gelu_pull(matmul_nt(grad_outer, outer_mat))
    grad_inner_low = grad_inner.astype(jnp.bfloat16)
    inner_mat_grad = matmul_tn(hidden_low, grad_inner_low)
    inner_vec_grad = column_sums(grad_inner_low)
    grad_hidden = grad_two + matmul_nt(grad_inner_low, inner_mat)
    grad_one, first_gain_grad, first_shift_grad = first_pull(grad_hidden)
    grad_attn = grad_one.astype(jnp.bfloat16)
    output_mat_grad = matmul_tn(context_rows, grad_attn)
    output_vec_grad = column_sums(grad_attn)
    grad_context = (
        matmul_nt(grad_attn, output_mat).astype(jnp.bfloat16).reshape(frame_count, HEADS, head_size)
    )
    scores = block_scores(query_heads, key_heads, groups, groups, score_scale)
    attn_prob = jnp.exp(scores - log_totals)
    grad_prob = jnp.einsum(
        "qhd,khd->hqk", grad_context, value_heads, preferred_element_type=jnp.float32
    )
    inner_sum = jnp.sum(attn_prob * grad_prob, axis=-1, keepdims=True)
    grad_scores = (attn_prob * (grad_prob - inner_sum)).astype(jnp.bfloat16)
    query_grad_parts = (
        jnp.einsum("hqk,khd->qhd", grad_scores, key_heads, preferred_element_type=jnp.float32)
        * score_scale
    )
    key_grad_sum = (
        jnp.einsum("hqk,qhd->khd", grad_scores, query_heads, preferred_element_type=jnp.float32)
        * score_scale
    )
    value_grad_sum = jnp.einsum(
        "hqk,qhd->khd",
        attn_prob.astype(jnp.bfloat16),
        grad_context,
        preferred_element_type=jnp.float32,
    )
    grad_query = query_grad_parts.reshape(frame_count, model_width).astype(jnp.bfloat16)
    grad_key = key_grad_sum.reshape(frame_count, model_width).astype(jnp.bfloat16)
    grad_value = value_grad_sum.reshape(frame_count, model_width).astype(jnp.bfloat16)
    query_mat_grad = matmul_tn(frames, grad_query)
    query_vec_grad = column_sums(grad_query)
    key_mat_grad = matmul_tn(frames, grad_key)
    value_mat_grad = matmul_tn(frames, grad_value)
    value_vec_grad = column_sums(grad_value)
    frames_grad = (
        grad_one
        + matmul_nt(grad_query, query_mat)
        + matmul_nt(grad_key, key_mat)
        + matmul_nt(grad_value, value_mat)
    ).astype(jnp.bfloat16)
    shares = (
        lax.psum_scatter(query_mat_grad, ("dp", "fsdp"), scatter_dimension=0, tiled=True),
        lax.psum_scatter(query_vec_grad, ("dp", "fsdp"), scatter_dimension=0, tiled=True),
        lax.psum_scatter(key_mat_grad, ("dp", "fsdp"), scatter_dimension=0, tiled=True),
        lax.psum_scatter(value_mat_grad, ("dp", "fsdp"), scatter_dimension=0, tiled=True),
        lax.psum_scatter(value_vec_grad, ("dp", "fsdp"), scatter_dimension=0, tiled=True),
        lax.psum_scatter(output_mat_grad, ("dp", "fsdp"), scatter_dimension=0, tiled=True),
        lax.psum_scatter(output_vec_grad, ("dp", "fsdp"), scatter_dimension=0, tiled=True),
        lax.psum_scatter(first_gain_grad, ("dp", "fsdp"), scatter_dimension=0, tiled=True),
        lax.psum_scatter(first_shift_grad, ("dp", "fsdp"), scatter_dimension=0, tiled=True),
        lax.psum_scatter(inner_mat_grad, ("dp", "fsdp"), scatter_dimension=0, tiled=True),
        lax.psum_scatter(inner_vec_grad, ("dp", "fsdp"), scatter_dimension=0, tiled=True),
        lax.psum_scatter(outer_mat_grad, ("dp", "fsdp"), scatter_dimension=0, tiled=True),
        lax.psum_scatter(outer_vec_grad, ("dp", "fsdp"), scatter_dimension=0, tiled=True),
        lax.psum_scatter(second_gain_grad, ("dp", "fsdp"), scatter_dimension=0, tiled=True),
        lax.psum_scatter(second_shift_grad, ("dp", "fsdp"), scatter_dimension=0, tiled=True),
    )
    return (
        layer_out,
        frames_grad,
        shares[0],
        shares[1],
        shares[2],
        shares[3],
        shares[4],
        shares[5],
        shares[6],
        shares[7],
        shares[8],
        shares[9],
        shares[10],
        shares[11],
        shares[12],
        shares[13],
        shares[14],
    )


def solution(mesh):
    in_specs = (
        P(("dp", "fsdp"), None),
        P(("dp", "fsdp"), None),
        P(("dp", "fsdp"), None),
        P(("dp", "fsdp")),
        P(("dp", "fsdp"), None),
        P(("dp", "fsdp"), None),
        P(("dp", "fsdp")),
        P(("dp", "fsdp"), None),
        P(("dp", "fsdp")),
        P(("dp", "fsdp")),
        P(("dp", "fsdp")),
        P(("dp", "fsdp"), None),
        P(("dp", "fsdp")),
        P(("dp", "fsdp"), None),
        P(("dp", "fsdp")),
        P(("dp", "fsdp")),
        P(("dp", "fsdp")),
        P(("dp", "fsdp"), None),
    )
    out_specs = (
        P(("dp", "fsdp"), None),
        P(("dp", "fsdp"), None),
        P(("dp", "fsdp"), None),
        P(("dp", "fsdp")),
        P(("dp", "fsdp"), None),
        P(("dp", "fsdp"), None),
        P(("dp", "fsdp")),
        P(("dp", "fsdp"), None),
        P(("dp", "fsdp")),
        P(("dp", "fsdp")),
        P(("dp", "fsdp")),
        P(("dp", "fsdp"), None),
        P(("dp", "fsdp")),
        P(("dp", "fsdp"), None),
        P(("dp", "fsdp")),
        P(("dp", "fsdp")),
        P(("dp", "fsdp")),
    )
    return jax.shard_map(
        per_device, mesh=mesh, in_specs=in_specs, out_specs=out_specs, check_vma=False
    )
```

profile of v0, /device:TPU:0, one launch (start us, length us, event | category | flops | bytes accessed | tf_op | source)
XLA Modules:
  0.0 1126.2 jit_solution(8192119810610155402)
XLA Ops:
  18.8 42.6 %all-reduce.19 = (bf16[768]{0:T(1024)(128)(2,1)S(1)}, bf16[768]{0:T(1024)(128)(2,1)S(1)}, bf16[768]{0:T(1024)(128)(2,1)S(1)}, bf16[768]{0:T(1024)(128)(2,1)S(1)}...) all-reduce(bf16[768]{0:T(1024)(128)(2,1)S(1)} %dynamic-update-slice, ...), channel_id=1, replica_groups=mesh['dp'=4,'fsdp'=8] {'dp','fsdp'}, use_global_device_ids=true, to_apply=%add | all-reduce | flops 9216 | bytes 36864
  63.8 4.3 all-gather.7.cloned.1.call-done
  70.4 54.0 %all-gather.9.cloned.1.call-done = bf16[768,768]{1,0:T(8,128)(2,1)} async-done(((bf16[24,768]{1,0:T(8,128)(2,1)}), bf16[768,768]{1,0:T(8,128)(2,1)}) %all-gather.9.cloned.1.call-update) | async-done | bytes 1179664 | tf_op jit(solution)/shard_map/all_gather | solution.py:77
  124.4 2.9 add_convert_fusion.2
  129.3 51.2 %all-gather.11.cloned.1.call-done = bf16[768,768]{1,0:T(8,128)(2,1)} async-done(((bf16[24,768]{1,0:T(8,128)(2,1)}), bf16[768,768]{1,0:T(8,128)(2,1)}) %all-gather.11.cloned.1.call-update) | async-done | bytes 1179664 | tf_op jit(solution)/shard_map/all_gather | solution.py:79
  180.5 2.9 convolution_convert_fusion.1
  186.9 2.6 fusion
  191.5 4.4 fusion.18
  195.8 40.6 %all-gather.13.cloned.1.call-done = bf16[768,768]{1,0:T(8,128)(2,1)} async-done(((bf16[24,768]{1,0:T(8,128)(2,1)}), bf16[768,768]{1,0:T(8,128)(2,1)}) %all-gather.13.cloned.1.call-update) | async-done | bytes 1179664 | tf_op jit(solution)/shard_map/all_gather | solution.py:82
  236.5 2.4 fusion.35
  240.4 61.6 %all-gather.15.cloned.1.call-done = bf16[768,3072]{1,0:T(8,128)(2,1)} async-done(((bf16[24,3072]{1,0:T(8,128)(2,1)}), bf16[768,3072]{1,0:T(8,128)(2,1)}) %all-gather.15.cloned.1.call-update) | async-done | bytes 4718608 | tf_op jit(solution)/shard_map/all_gather | solution.py:86
  301.9 21.0 %multiply_convert_fusion.1 = (bf16[512,3072]{1,0:T(8,128)(2,1)}, f32[512,3072]{1,0:T(8,128)}, f32[512,3072]{1,0:T(8,128)}) fusion(f32[3072]{0:T(1024)S(1)} %convert_element_type.159, bf16[768,3072]{1,0:T(8,128)(2,1)} %all-gather.15.cloned.1.call-done, f32[512,768]{1,0:T(8,128)} %copy-done.7, f32[768]{0:T(1024)S(1)} %convert_element_type.157, ...), kind=kOutput, calls=%fused_computation.14 | convolution fusion | flops 2521694208 | bytes 22042624 | tf_op jit(solution)/shard_map/dot_general | solution.py:20
  322.9 44.4 %all-gather.17.cloned.1.call-done = bf16[3072,768]{1,0:T(8,128)(2,1)} async-done(((bf16[96,768]{1,0:T(8,128)(2,1)}), bf16[3072,768]{1,0:T(8,128)(2,1)}) %all-gather.17.cloned.1.call-update) | async-done | bytes 4718608 | tf_op jit(solution)/shard_map/all_gather | solution.py:88
  367.3 6.1 fusion.36
  377.2 8.5 convert_reduce_fusion
  385.7 3.1 multiply_reduce_fusion.2
  394.7 13.5 %multiply_reduce_fusion = (f32[12,512]{1,0:T(8,128)S(1)}, f32[12,512,512]{1,2,0:T(8,128)}) fusion(f32[12,512]{1,0:T(8,128)S(1)} %log_add_fusion, f32[12,512,512]{1,2,0:T(8,128)} %copy-done, pred[512,512]{0,1:T(8,128)(4,1)S(1)} %broadcast_compare_fusion, bf16[512,12,64]{0,2,1:T(8,128)(2,1)} %bitcast.82, bf16[512,12,64]{0,2,1:T(8,128)(2,1)} %bitcast.81), kind=kOutput, calls=%fused_computation.1 | convolution fusion | flops 418375680 | bytes 27049984 | tf_op jit(solution)/shard_map/qhd,khd->hqk/dot_general | solution.py:174
  408.3 7.0 multiply_convert_fusion
  421.0 3.1 copy.87
  424.4 4.8 multiply_convert_fusion.2
  432.3 3.2 copy.89
  435.6 6.6 convert_reduce_fusion.3
  445.3 3.2 copy.91
  448.6 3.7 fusion.39
  452.4 7.2 fusion.28
  460.8 8.2 fusion.40
  469.2 40.8 %all-reduce.18 = (f32[768]{0:T(1024)S(1)}, f32[768]{0:T(1024)S(1)}, f32[768]{0:T(1024)S(1)}, f32[768]{0:T(1024)S(1)}, f32[768]{0:T(1024)S(1)}, /*index=5*/f32[30...) all-reduce(f32[768]{0:T(1024)S(1)} %reduce_sum.228, ...), channel_id=3, replica_groups=mesh['dp'=4,'fsdp'=8] {'dp','fsdp'}, use_global_device_ids=true, to_apply=%region_15.16.clone | all-reduce | flops 9216 | bytes 73728
  522.3 104.8 %reduce-scatter.21.cloned.1.call-done = f32[24,768]{1,0:T(8,128)} async-done(((f32[768,768]{1,0:T(8,128)}), f32[24,768]{1,0:T(8,128)}) %reduce-scatter.21.cloned.1.call-update) | async-done | bytes 73744
  627.1 103.9 %reduce-scatter.23.cloned.1.call-done = f32[24,768]{1,0:T(8,128)} async-done(((f32[768,768]{1,0:T(8,128)}), f32[24,768]{1,0:T(8,128)}) %reduce-scatter.23.cloned.1.call-update) | async-done | bytes 73744
  731.0 104.7 %reduce-scatter.13.cloned.1.call-done = f32[24,768]{1,0:T(8,128)} async-done(((f32[768,768]{1,0:T(8,128)}), f32[24,768]{1,0:T(8,128)}) %reduce-scatter.13.cloned.1.call-update) | async-done | bytes 73744 | tf_op jit(solution)/shard_map/reduce_scatter | solution.py:213
  835.7 141.2 %reduce-scatter.15.cloned.1.call-done = f32[24,3072]{1,0:T(8,128)} async-done(((f32[768,3072]{1,0:T(8,128)}), f32[24,3072]{1,0:T(8,128)}) %reduce-scatter.15.cloned.1.call-update) | async-done | bytes 294928 | tf_op jit(solution)/shard_map/reduce_scatter | solution.py:217
  976.8 142.0 %reduce-scatter.17.cloned.1.call-done = f32[96,768]{1,0:T(8,128)} async-done(((f32[3072,768]{1,0:T(8,128)}), f32[96,768]{1,0:T(8,128)}) %reduce-scatter.17.cloned.1.call-update) | async-done | bytes 294928 | tf_op jit(solution)/shard_map/reduce_scatter | solution.py:219
  (162 shorter events, 60.5 us)
Async XLA Ops:
  7.2 117.2 %copy-start.2 = (bf16[512,768]{1,0:T(8,128)(2,1)S(1)}, bf16[512,768]{1,0:T(8,128)(2,1)}, u32[]{:S(2)}) copy-start(bf16[512,768]{1,0:T(8,128)(2,1)} %param.18) | copy-start | bytes 2359300
  7.2 60.9 %all-gather.7.cloned.1.call-start = ((), (), s32[]{:S(2)}) async-start(), calls=%async_computation.6 | async-start | bytes 1216512 | tf_op jit(solution)/shard_map/all_gather | solution.py:80
  7.9 116.4 %all-gather.9.cloned.1.call-start = ((), (), s32[]{:S(2)}) async-start(), calls=%async_computation.7 | async-start | bytes 1216512 | tf_op jit(solution)/shard_map/all_gather | solution.py:77
  8.7 171.8 %all-gather.11.cloned.1.call-start = ((), (), s32[]{:S(2)}) async-start(), calls=%async_computation.8 | async-start | bytes 1216512 | tf_op jit(solution)/shard_map/all_gather | solution.py:79
  9.4 227.0 %all-gather.13.cloned.1.call-start = ((), (), s32[]{:S(2)}) async-start(), calls=%async_computation.9 | async-start | bytes 1216512 | tf_op jit(solution)/shard_map/all_gather | solution.py:82
  10.0 292.0 %all-gather.15.cloned.1.call-start = ((), (), s32[]{:S(2)}) async-start(), calls=%async_computation.10 | async-start | bytes 4866048 | tf_op jit(solution)/shard_map/all_gather | solution.py:86
  10.6 356.7 %all-gather.17.cloned.1.call-start = ((), (), s32[]{:S(2)}) async-start(), calls=%async_computation.11 | async-start | bytes 4866048 | tf_op jit(solution)/shard_map/all_gather | solution.py:88
  11.2 511.1 %reduce-scatter.19.cloned.1.call-start = ((), (), s32[]{:S(2)}) async-start(), calls=%async_computation.15 | async-start | bytes 2433024
  127.6 61.9 %copy-start.11 = (bf16[512,768]{0,1:T(8,128)(2,1)}, bf16[512,768]{0,1:T(8,128)(2,1)S(1)}, u32[]{:S(2)}) copy-start(bf16[512,768]{0,1:T(8,128)(2,1)S(1)} %copy.72) | copy-start | bytes 2359300
  186.9 4.6 copy-start
  240.4 126.9 %copy-start.8 = (f32[512,768]{1,0:T(8,128)S(1)}, f32[512,768]{1,0:T(8,128)}, u32[]{:S(2)}) copy-start(f32[512,768]{1,0:T(8,128)} %copy-done.7) | copy-start | bytes 4718596
  367.3 6.4 copy-start.13
  376.3 9.4 slice-start.3
  376.5 9.2 copy-start.20
  377.2 8.5 slice-start.4
  385.7 3.2 copy-start.25
  385.7 3.2 copy-start.9
  394.7 13.5 %slice-start = ((s8[12582912]{0:T(1024)(128)(4,1)}), s8[4194304]{0:T(1024)(128)(4,1)S(1)}, s32[]{:S(2)}) async-start(s8[12582912]{0:T(1024)(128)(4,1)} %bitcast.72), calls=%async_computation.18 | async-start | bytes 8388608
  394.7 13.5 %slice-start.1 = ((s8[12582912]{0:T(1024)(128)(4,1)}), s8[4194304]{0:T(1024)(128)(4,1)S(1)}, s32[]{:S(2)}) async-start(s8[12582912]{0:T(1024)(128)(4,1)} %bitcast.72), calls=%async_computation.19 | async-start | bytes 8388608
  394.7 13.5 %slice-start.2 = ((s8[12582912]{0:T(1024)(128)(4,1)}), s8[4194304]{0:T(1024)(128)(4,1)S(1)}, s32[]{:S(2)}) async-start(s8[12582912]{0:T(1024)(128)(4,1)} %bitcast.72), calls=%async_computation.20 | async-start | bytes 8388608
  415.3 3.5 copy-start.3
  424.1 6.0 copy-start.4
  424.1 203.0 %reduce-scatter.21.cloned.1.call-start = ((), (), s32[]{:S(2)}) async-start(), calls=%async_computation.16 | async-start | bytes 2433024
  432.3 3.3 copy-start.12
  435.5 295.5 %reduce-scatter.23.cloned.1.call-start = ((), (), s32[]{:S(2)}) async-start(), calls=%async_computation.17 | async-start | bytes 2433024
  448.5 3.8 copy-start.10
  448.5 387.1 %reduce-scatter.13.cloned.1.call-start = ((), (), s32[]{:S(2)}) async-start(), calls=%async_computation.12 | async-start | bytes 2433024 | tf_op jit(solution)/shard_map/reduce_scatter | solution.py:213
  452.3 524.5 %reduce-scatter.15.cloned.1.call-start = ((), (), s32[]{:S(2)}) async-start(), calls=%async_computation.13 | async-start | bytes 9732096 | tf_op jit(solution)/shard_map/reduce_scatter | solution.py:217
  459.6 659.2 %reduce-scatter.17.cloned.1.call-start = ((), (), s32[]{:S(2)}) async-start(), calls=%async_computation.14 | async-start | bytes 9732096 | tf_op jit(solution)/shard_map/reduce_scatter | solution.py:219
  469.0 46.3 %copy-start.18 = (bf16[12,64,512]{2,1,0:T(8,128)(2,1)S(1)}, bf16[12,64,512]{2,1,0:T(8,128)(2,1)}, u32[]{:S(2)}) copy-start(bf16[12,64,512]{2,1,0:T(8,128)(2,1)} %copy-done.17) | copy-start | bytes 2359300
  469.0 48.5 %copy-start.6 = (bf16[12,64,512]{2,1,0:T(8,128)(2,1)S(1)}, bf16[12,64,512]{2,1,0:T(8,128)(2,1)}, u32[]{:S(2)}) copy-start(bf16[12,64,512]{2,1,0:T(8,128)(2,1)} %copy-done.5) | copy-start | bytes 2359300
  510.0 7.5 copy-start.23
  (11 other events, 19.1 us)
Sparse Core Ops, SparseCore 0:
  11.0 57.0 all-gather.6
  71.1 53.2 all-gather.8
  127.4 53.0 all-gather.10
  183.3 53.0 all-gather.12
  239.3 62.6 all-gather.14
  304.8 62.4 all-gather.16
  424.2 98.0 reduce-scatter.18
  529.0 98.0 reduce-scatter.20
  632.9 98.0 reduce-scatter.22
  737.6 98.0 reduce-scatter.12
  842.1 134.6 reduce-scatter.14
  984.2 134.6 reduce-scatter.16
where the time goes:
time: 1140 us; the launch traced here: 1130 us
  waiting for transfers between devices  858 us (75%)
  matrix products  114 us (10%)
  blocking collectives  83.4 us (7%)
  local copies, waits for them, and re-layouts  38.6 us (3%)
  other arithmetic  15.6 us (1%)
  between operations  15.2 us (1%)
    unnamed x15, waiting for transfers between devices  214 us
    reduce_scatter x1, waiting for transfers between devices, per_device(): lax.psum_scatter(outer_mat_grad, ('dp', 'fsdp'), scatter_dimension=0, til...  142 us
    reduce_scatter x1, waiting for transfers between devices, per_device(): lax.psum_scatter(inner_mat_grad, ('dp', 'fsdp'), scatter_dimension=0, til...  141 us
    reduce_scatter x1, waiting for transfers between devices, per_device(): lax.psum_scatter(output_mat_grad, ('dp', 'fsdp'), scatter_dimension=0, ti...  105 us
    unnamed x2, blocking collectives  83.4 us
    all_gather x1, waiting for transfers between devices, per_device(): lax.all_gather(inner_weight, ('dp', 'fsdp'), axis=0, tiled=True)  61.6 us
    all_gather x1, waiting for transfers between devices, per_device(): lax.all_gather(query_weight, ('dp', 'fsdp'), axis=0, tiled=True)  54 us
    all_gather x1, waiting for transfers between devices, per_device(): lax.all_gather(key_weight, ('dp', 'fsdp'), axis=0, tiled=True)  51.2 us
  transfers between devices with their start and end apart: 12, of which 12 were waited for; matrix products, arithmetic and copies ran while one was open for 9% of the time, Pallas kernels for 0%

commit v1 on v0

--- a/solution.py
+++ b/solution.py
@@ -4,6 +4,18 @@
 from jax.sharding import PartitionSpec as P
 
 HEADS = 12
+
+
+def collect(array, axis, dim):
+    ways, here = (lax.axis_size(axis), lax.axis_index(axis))
+    grown, reach = (array, 1)
+    while reach < ways:
+        theirs = lax.ppermute(grown, axis, [(d, d ^ reach) for d in range(ways)])
+        mine_first = jnp.concatenate([grown, theirs], axis=dim)
+        theirs_first = jnp.concatenate([theirs, grown], axis=dim)
+        grown = jnp.where(here & reach == 0, mine_first, theirs_first)
+        reach = 2 * reach
+    return grown
 
 
 def layer_norm(values, gain_vec, shift_vec):
@@ -79,7 +91,7 @@
         lax.all_gather(key_weight, ("dp", "fsdp"), axis=0, tiled=True),
         lax.all_gather(value_weight, ("dp", "fsdp"), axis=0, tiled=True),
         lax.all_gather(value_bias, ("dp", "fsdp"), axis=0, tiled=True),
-        lax.all_gather(output_weight, ("dp", "fsdp"), axis=0, tiled=True),
+        collect(output_weight, ("dp", "fsdp"), 0),
         lax.all_gather(output_bias, ("dp", "fsdp"), axis=0, tiled=True),
         lax.all_gather(first_gain, ("dp", "fsdp"), axis=0, tiled=True),
         lax.all_gather(first_shift, ("dp", "fsdp"), axis=0, tiled=True),

time: 1140 us -> 1110 us (0.974)
  waiting for transfers between devices: 858 us -> 827 us
    all_gather x1, waiting for transfers between devices: 61.6 us -> 46.7 us  [per_device(): lax.all_gather(inner_weight, ('dp', 'fsdp'), axis=0, tiled=True)]
    all_gather x1, waiting for transfers between devices: 54 us -> 42 us  [per_device(): lax.all_gather(query_weight, ('dp', 'fsdp'), axis=0, tiled=True)]
    unnamed x92 -> x90, local copies, waits for them, and re-layouts: 32.1 us -> 31.2 us
  transfers between devices with their start and end apart: 12 -> 17, of which waited for: 12 -> 14; matrix products, arithmetic and copies ran while one was open for 9% -> 12% of each run, Pallas kernels for 0% -> 0%
where the time goes in v1:
time: 1110 us; the launch traced here: 1100 us
  waiting for transfers between devices  827 us (75%)
  matrix products  115 us (10%)
  blocking collectives  81.8 us (7%)
  local copies, waits for them, and re-layouts  36.2 us (3%)
  other arithmetic  18.4 us (2%)
  between operations  15.2 us (1%)
  starting transfers between devices  11.4 us (1%)
    unnamed x15, waiting for transfers between devices  215 us
    reduce_scatter x1, waiting for transfers between devices, per_device(): lax.psum_scatter(outer_mat_grad, ('dp', 'fsdp'), scatter_dimension=0, til...  142 us
    reduce_scatter x1, waiting for transfers between devices, per_device(): lax.psum_scatter(inner_mat_grad, ('dp', 'fsdp'), scatter_dimension=0, til...  141 us
    reduce_scatter x1, waiting for transfers between devices, per_device(): lax.psum_scatter(output_mat_grad, ('dp', 'fsdp'), scatter_dimension=0, ti...  105 us
    unnamed x2, blocking collectives  81.8 us
    all_gather x1, waiting for transfers between devices, per_device(): lax.all_gather(key_weight, ('dp', 'fsdp'), axis=0, tiled=True)  53.8 us
    all_gather x1, waiting for transfers between devices, per_device(): lax.all_gather(inner_weight, ('dp', 'fsdp'), axis=0, tiled=True)  46.7 us
    all_gather x1, waiting for transfers between devices, per_device(): lax.all_gather(outer_weight, ('dp', 'fsdp'), axis=0, tiled=True)  44.4 us
  transfers between devices with their start and end apart: 17, of which 14 were waited for; matrix products, arithmetic and copies ran while one was open for 12% of the time, Pallas kernels for 0%

profile of v1, /device:TPU:0, one launch (start us, length us, event | category | flops | bytes accessed | tf_op | source)
XLA Modules:
  0.0 1104.5 jit_solution(8416821745512684951)
XLA Ops:
  10.6 3.0 collective-permute-start
  21.2 3.1 collective-permute-start.2
  31.9 41.2 %all-reduce.19 = (bf16[768]{0:T(1024)(128)(2,1)S(1)}, bf16[768]{0:T(1024)(128)(2,1)S(1)}, bf16[768]{0:T(1024)(128)(2,1)S(1)}, bf16[768]{0:T(1024)(128)(2,1)S(1)}...) all-reduce(bf16[768]{0:T(1024)(128)(2,1)S(1)} %dynamic-update-slice, ...), channel_id=1, replica_groups=mesh['dp'=4,'fsdp'=8] {'dp','fsdp'}, use_global_device_ids=true, to_apply=%add | all-reduce | flops 9216 | bytes 36864
  82.3 42.0 %all-gather.9.cloned.1.call-done = bf16[768,768]{1,0:T(8,128)(2,1)} async-done(((bf16[24,768]{1,0:T(8,128)(2,1)}), bf16[768,768]{1,0:T(8,128)(2,1)}) %all-gather.9.cloned.1.call-update) | async-done | bytes 1179664 | tf_op jit(solution)/shard_map/all_gather | solution.py:89
  126.6 53.8 %all-gather.11.cloned.1.call-done = bf16[768,768]{1,0:T(8,128)(2,1)} async-done(((bf16[24,768]{1,0:T(8,128)(2,1)}), bf16[768,768]{1,0:T(8,128)(2,1)}) %all-gather.11.cloned.1.call-update) | async-done | bytes 1179664 | tf_op jit(solution)/shard_map/all_gather | solution.py:91
  180.4 2.9 convolution_convert_fusion.1
  191.4 3.6 fusion.18
  195.0 2.8 fusion.42
  199.3 46.7 %all-gather.13.cloned.1.call-done = bf16[768,3072]{1,0:T(8,128)(2,1)} async-done(((bf16[24,3072]{1,0:T(8,128)(2,1)}), bf16[768,3072]{1,0:T(8,128)(2,1)}) %all-gather.13.cloned.1.call-update) | async-done | bytes 4718608 | tf_op jit(solution)/shard_map/all_gather | solution.py:98
  246.0 20.9 %multiply_convert_fusion.1 = (bf16[512,3072]{1,0:T(8,128)(2,1)}, f32[512,3072]{1,0:T(8,128)}, f32[512,3072]{1,0:T(8,128)}) fusion(f32[3072]{0:T(1024)S(1)} %convert_element_type.159, bf16[768,3072]{1,0:T(8,128)(2,1)} %all-gather.13.cloned.1.call-done, f32[512,768]{1,0:T(8,128)} %copy-done.7, f32[768]{0:T(1024)S(1)} %convert_element_type.157, ...), kind=kOutput, calls=%fused_computation.14 | convolution fusion | flops 2521694208 | bytes 22042624 | tf_op jit(solution)/shard_map/dot_general | solution.py:32
  266.9 44.4 %all-gather.15.cloned.1.call-done = bf16[3072,768]{1,0:T(8,128)(2,1)} async-done(((bf16[96,768]{1,0:T(8,128)(2,1)}), bf16[3072,768]{1,0:T(8,128)(2,1)}) %all-gather.15.cloned.1.call-update) | async-done | bytes 4718608 | tf_op jit(solution)/shard_map/all_gather | solution.py:100
  311.3 6.1 fusion.43
  321.2 8.5 convert_reduce_fusion
  329.8 3.2 multiply_reduce_fusion.2
  334.7 32.5 %all-gather.17.cloned.1.call-done = bf16[768,768]{1,0:T(8,128)(2,1)} async-done(((bf16[24,768]{1,0:T(8,128)(2,1)}), bf16[768,768]{1,0:T(8,128)(2,1)}) %all-gather.17.cloned.1.call-update) | async-done | bytes 1179664 | tf_op jit(solution)/shard_map/all_gather | solution.py:162
  367.2 3.2 convolution_convert_fusion
  372.7 13.5 %multiply_reduce_fusion = (f32[12,512]{1,0:T(8,128)S(1)}, f32[12,512,512]{1,2,0:T(8,128)}) fusion(f32[12,512]{1,0:T(8,128)S(1)} %log_add_fusion, f32[12,512,512]{1,2,0:T(8,128)} %copy-done, pred[512,512]{0,1:T(8,128)(4,1)S(1)} %broadcast_compare_fusion, bf16[512,12,64]{0,2,1:T(8,128)(2,1)} %bitcast.81, bf16[512,12,64]{0,2,1:T(8,128)(2,1)} %bitcast.80), kind=kOutput, calls=%fused_computation.1 | convolution fusion | flops 418375680 | bytes 27049984 | tf_op jit(solution)/shard_map/qhd,khd->hqk/dot_general | solution.py:186
  386.3 7.0 multiply_convert_fusion
  399.0 3.1 copy.87
  402.4 4.8 multiply_convert_fusion.2
  410.3 3.2 copy.89
  413.6 6.6 convert_reduce_fusion.3
  423.3 3.2 copy.91
  426.5 3.7 fusion.46
  430.3 7.3 fusion.35
  438.7 8.2 fusion.47
  447.1 40.6 %all-reduce.18 = (f32[768]{0:T(1024)S(1)}, f32[768]{0:T(1024)S(1)}, f32[768]{0:T(1024)S(1)}, f32[768]{0:T(1024)S(1)}, f32[768]{0:T(1024)S(1)}, /*index=5*/f32[30...) all-reduce(f32[768]{0:T(1024)S(1)} %reduce_sum.228, ...), channel_id=3, replica_groups=mesh['dp'=4,'fsdp'=8] {'dp','fsdp'}, use_global_device_ids=true, to_apply=%region_15.16.clone | all-reduce | flops 9216 | bytes 73728
  500.8 104.7 %reduce-scatter.21.cloned.1.call-done = f32[24,768]{1,0:T(8,128)} async-done(((f32[768,768]{1,0:T(8,128)}), f32[24,768]{1,0:T(8,128)}) %reduce-scatter.21.cloned.1.call-update) | async-done | bytes 73744
  605.5 103.9 %reduce-scatter.23.cloned.1.call-done = f32[24,768]{1,0:T(8,128)} async-done(((f32[768,768]{1,0:T(8,128)}), f32[24,768]{1,0:T(8,128)}) %reduce-scatter.23.cloned.1.call-update) | async-done | bytes 73744
  709.4 104.7 %reduce-scatter.13.cloned.1.call-done = f32[24,768]{1,0:T(8,128)} async-done(((f32[768,768]{1,0:T(8,128)}), f32[24,768]{1,0:T(8,128)}) %reduce-scatter.13.cloned.1.call-update) | async-done | bytes 73744 | tf_op jit(solution)/shard_map/reduce_scatter | solution.py:225
  814.0 141.0 %reduce-scatter.15.cloned.1.call-done = f32[24,3072]{1,0:T(8,128)} async-done(((f32[768,3072]{1,0:T(8,128)}), f32[24,3072]{1,0:T(8,128)}) %reduce-scatter.15.cloned.1.call-update) | async-done | bytes 294928 | tf_op jit(solution)/shard_map/reduce_scatter | solution.py:229
  955.0 142.1 %reduce-scatter.17.cloned.1.call-done = f32[96,768]{1,0:T(8,128)} async-done(((f32[3072,768]{1,0:T(8,128)}), f32[96,768]{1,0:T(8,128)}) %reduce-scatter.17.cloned.1.call-update) | async-done | bytes 294928 | tf_op jit(solution)/shard_map/reduce_scatter | solution.py:231
  (174 shorter events, 73.9 us)
Async XLA Ops:
  7.2 72.5 %all-gather.7.cloned.1.call-start = ((), (), s32[]{:S(2)}) async-start(), calls=%async_computation.6 | async-start | bytes 1216512 | tf_op jit(solution)/shard_map/all_gather | solution.py:92
  7.9 116.3 %all-gather.9.cloned.1.call-start = ((), (), s32[]{:S(2)}) async-start(), calls=%async_computation.7 | async-start | bytes 1216512 | tf_op jit(solution)/shard_map/all_gather | solution.py:89
  8.7 171.7 %all-gather.11.cloned.1.call-start = ((), (), s32[]{:S(2)}) async-start(), calls=%async_computation.8 | async-start | bytes 1216512 | tf_op jit(solution)/shard_map/all_gather | solution.py:91
  9.4 236.6 %all-gather.13.cloned.1.call-start = ((), (), s32[]{:S(2)}) async-start(), calls=%async_computation.9 | async-start | bytes 4866048 | tf_op jit(solution)/shard_map/all_gather | solution.py:98
  10.0 301.3 %all-gather.15.cloned.1.call-start = ((), (), s32[]{:S(2)}) async-start(), calls=%async_computation.10 | async-start | bytes 4866048 | tf_op jit(solution)/shard_map/all_gather | solution.py:100
  10.6 356.6 %all-gather.17.cloned.1.call-start = ((), (), s32[]{:S(2)}) async-start(), calls=%async_computation.11 | async-start | bytes 1216512 | tf_op jit(solution)/shard_map/all_gather | solution.py:162
  10.6 5.2 collective-permute-start
  16.6 4.5 collective-permute-start.1
  21.2 53.5 %collective-permute-start.2 = (bf16[96,768]{1,0:T(8,128)(2,1)S(1)}, bf16[96,768]{1,0:T(8,128)(2,1)S(1)}, u32[]{:S(2)}, u32[]{:S(2)}) collective-permute-start(bf16[96,768]{1,0:T(8,128)(2,1)S(1)} %maximum_select_fusion.4), channel_id=1, source_target_pairs={{0,4},{1,5},{2,6},{3,7},{4,0},{5,1},{6,2},{7,3},{8,12},{9,13},{10,... | collective-permute-start | bytes 442376 | tf_op jit(solution)/shard_map/ppermute | solution.py:13
  24.3 476.5 %reduce-scatter.19.cloned.1.call-start = ((), (), s32[]{:S(2)}) async-start(), calls=%async_computation.15 | async-start | bytes 2433024
  74.7 1.6 collective-permute-start.3
  77.4 46.9 %copy-start.2 = (bf16[512,768]{1,0:T(8,128)(2,1)S(1)}, bf16[512,768]{1,0:T(8,128)(2,1)}, u32[]{:S(2)}) copy-start(bf16[512,768]{1,0:T(8,128)(2,1)} %param.18) | copy-start | bytes 2359300
  77.4 117.6 %collective-permute-start.4 = (bf16[384,768]{1,0:T(8,128)(2,1)}, bf16[384,768]{1,0:T(8,128)(2,1)}, u32[]{:S(2)}, u32[]{:S(2)}) collective-permute-start(bf16[384,768]{1,0:T(8,128)(2,1)} %maximum_select_fusion.2), channel_id=1, source_target_pairs={{0,16},{1,17},{2,18},{3,19},{4,20},{5,21},{6,22},{7,23},{8,24},{9,... | collective-permute-start | bytes 1769480 | tf_op jit(solution)/shard_map/ppermute | solution.py:13
  82.3 107.1 %copy-start.11 = (bf16[512,768]{0,1:T(8,128)(2,1)}, bf16[512,768]{0,1:T(8,128)(2,1)S(1)}, u32[]{:S(2)}) copy-start(bf16[512,768]{0,1:T(8,128)(2,1)S(1)} %copy.72) | copy-start | bytes 2359300
  186.8 4.6 copy-start
  199.3 112.1 %copy-start.8 = (f32[512,768]{1,0:T(8,128)S(1)}, f32[512,768]{1,0:T(8,128)}, u32[]{:S(2)}) copy-start(f32[512,768]{1,0:T(8,128)} %copy-done.7) | copy-start | bytes 4718596
  311.3 6.4 copy-start.13
  320.3 9.4 slice-start.3
  320.5 9.2 copy-start.19
  321.2 8.5 slice-start.4
  372.7 13.5 %slice-start = ((s8[12582912]{0:T(1024)(128)(4,1)}), s8[4194304]{0:T(1024)(128)(4,1)S(1)}, s32[]{:S(2)}) async-start(s8[12582912]{0:T(1024)(128)(4,1)} %bitcast.71), calls=%async_computation.18 | async-start | bytes 8388608
  372.7 13.5 %slice-start.1 = ((s8[12582912]{0:T(1024)(128)(4,1)}), s8[4194304]{0:T(1024)(128)(4,1)S(1)}, s32[]{:S(2)}) async-start(s8[12582912]{0:T(1024)(128)(4,1)} %bitcast.71), calls=%async_computation.19 | async-start | bytes 8388608
  372.7 13.5 %slice-start.2 = ((s8[12582912]{0:T(1024)(128)(4,1)}), s8[4194304]{0:T(1024)(128)(4,1)S(1)}, s32[]{:S(2)}) async-start(s8[12582912]{0:T(1024)(128)(4,1)} %bitcast.71), calls=%async_computation.20 | async-start | bytes 8388608
  402.1 6.0 copy-start.4
  402.1 203.4 %reduce-scatter.21.cloned.1.call-start = ((), (), s32[]{:S(2)}) async-start(), calls=%async_computation.16 | async-start | bytes 2433024
  413.5 295.9 %reduce-scatter.23.cloned.1.call-start = ((), (), s32[]{:S(2)}) async-start(), calls=%async_computation.17 | async-start | bytes 2433024
  426.5 387.6 %reduce-scatter.13.cloned.1.call-start = ((), (), s32[]{:S(2)}) async-start(), calls=%async_computation.12 | async-start | bytes 2433024 | tf_op jit(solution)/shard_map/reduce_scatter | solution.py:225
  430.3 524.8 %reduce-scatter.15.cloned.1.call-start = ((), (), s32[]{:S(2)}) async-start(), calls=%async_computation.13 | async-start | bytes 9732096 | tf_op jit(solution)/shard_map/reduce_scatter | solution.py:229
  437.6 659.6 %reduce-scatter.17.cloned.1.call-start = ((), (), s32[]{:S(2)}) async-start(), calls=%async_computation.14 | async-start | bytes 9732096 | tf_op jit(solution)/shard_map/reduce_scatter | solution.py:231
  446.9 46.0 %copy-start.17 = (bf16[12,64,512]{2,1,0:T(8,128)(2,1)S(1)}, bf16[12,64,512]{2,1,0:T(8,128)(2,1)}, u32[]{:S(2)}) copy-start(bf16[12,64,512]{2,1,0:T(8,128)(2,1)} %copy-done.16) | copy-start | bytes 2359300
  446.9 48.3 %copy-start.6 = (bf16[12,64,512]{2,1,0:T(8,128)(2,1)S(1)}, bf16[12,64,512]{2,1,0:T(8,128)(2,1)}, u32[]{:S(2)}) copy-start(bf16[12,64,512]{2,1,0:T(8,128)(2,1)} %copy-done.5) | copy-start | bytes 2359300
  487.7 7.5 copy-start.23
  (15 other events, 36.3 us)
Sparse Core Ops, SparseCore 0:
  11.0 57.0 all-gather.6
  71.1 53.1 all-gather.8
  127.3 53.0 all-gather.10
  183.2 62.6 all-gather.12
  248.8 62.4 all-gather.14
  314.2 52.9 all-gather.16
  402.2 98.5 reduce-scatter.18
  507.5 97.9 reduce-scatter.20
  611.4 97.9 reduce-scatter.22
  715.9 98.0 reduce-scatter.12
  820.5 134.4 reduce-scatter.14
  962.4 134.7 reduce-scatter.16
